TPU v7x, 32 devices: a whole 2x2x4 slice. The times are simulated.
32 devices in a mesh: seq: 8 (over z, x), head: 4 (over y, core).
Axes of the slice: x: 2, y: 2, z: 4, core: 2. Of those that a mesh axis runs over, the one named last changes fastest.
Arguments:
- queries: bfloat16 [8192, 4096], P('seq', 'head'), may hold values from -0.23925781 to 0.23925781
- keys: bfloat16 [8192, 4096], P('seq', 'head'), may hold values from -0.23925781 to 0.23925781
- values: bfloat16 [8192, 4096], P('seq', 'head'), may hold values from -1.5 to 1.5
- out_grad: bfloat16 [8192, 4096], P('seq', 'head'), may hold values from -1.5 to 1.5
- starts: int32 [8192], P('seq'), may hold values 0 or 1
- owners: int32 [8192, 1], P('seq'), may hold values from 0 to 3; in each aligned block of 1024 rows (0 to 1023, 1024 to 2047, ...) at most 512 rows name the same one
Outputs:
- returned: bfloat16 [16384, 3, 4096], P(('seq', 'head'))
Inputs may be any that keep to these rules, and one draw needn't show every extreme that they name: `owners`: among the 1024 tokens of one block, no owner is named by more than 512 tokens, a bound that some block reaches.
All inputs are finite; a program needn't handle non-finite values. No bound on the sum of `starts` on one device may be relied on, other than what follows from the above.
Results may differ from a plain program's by a relative error of at most 0.0049.
Values may be sent and summed in bfloat16 or wider, within the bound.
A program may use at most 128 MiB of HBM per device.

v0:
```python
import jax
import jax.numpy as jnp
from jax import lax
from jax.sharding import PartitionSpec as P

HD = 128


def entering(part, axis, combine, identity, reverse):
    count = lax.axis_size(axis)
    place = lax.axis_index(axis)
    ahead = count - 1 - place if reverse else place
    gathered = jax.tree.map(lambda a: lax.all_gather(a, axis), part)
    state = jax.tree.map(lambda a, e: jnp.zeros_like(a) + jnp.asarray(e, a.dtype), part, identity)

    def one(turn, state):
        source = count - 1 - turn if reverse else turn
        return combine(
            state, jax.tree.map(lambda a: lax.dynamic_index_in_dim(a, source, 0, False), gathered)
        )

    return lax.fori_loop(0, ahead, one, state)


def chain_combine(earlier, later):
    return (earlier[0] * later[0], later[1] + later[0] * earlier[1])


def place_rows(block, owners, count):
    span = block.shape[0]
    owner_ids = owners[:, 0]
    onehot = (owner_ids[:, None] == lax.iota(jnp.int32, count)[None, :]).astype(jnp.int32)
    before = jnp.cumsum(onehot, axis=0, dtype=jnp.int32) - onehot
    slots = jnp.sum(before * onehot, axis=1)
    capacity = 2 * span // count
    target = owner_ids * capacity + slots
    buffer = jnp.zeros((count * capacity,) + block.shape[1:], block.dtype).at[target].set(block)
    return buffer.reshape((count, capacity) + block.shape[1:])


def shards(queries, keys, values, out_grad, starts, owners):
    span, feats = queries.shape
    heads = feats // HD
    head_shape = (span, heads, HD)
    query_h = queries.reshape(head_shape)
    key_h = keys.reshape(head_shape)
    value_h = values.reshape(head_shape)
    grad_h = out_grad.reshape(head_shape)
    segment = jnp.cumsum(starts, dtype=jnp.int32)
    position = lax.iota(jnp.int32, span)
    allowed = (position[None, :] <= position[:, None]) & (segment[:, None] == segment[None, :])
    first = (segment == 0).astype(jnp.bfloat16)[:, None, None]
    last = (segment == segment[-1]).astype(jnp.bfloat16)[:, None, None]
    keep = (segment[-1] == 0).astype(jnp.float32).reshape(1, 1, 1)
    fwd_local = jnp.einsum(
        "thd,the->hde", key_h * last, value_h, preferred_element_type=jnp.float32
    )
    bwd_local = jnp.einsum(
        "thd,the->hde", query_h * first, grad_h, preferred_element_type=jnp.float32
    )
    zeros = jnp.zeros((heads, HD, HD), jnp.float32)
    unity = jnp.ones((1, 1, 1), jnp.float32)
    fwd_in = entering((keep, fwd_local), "seq", chain_combine, (unity, zeros), False)[1]
    bwd_in = entering((keep, bwd_local), "seq", chain_combine, (unity, zeros), True)[1]
    score_ov = jnp.einsum("thd,shd->hts", grad_h, value_h, preferred_element_type=jnp.float32)
    weight_ov = jnp.where(allowed[None], score_ov, 0.0).astype(jnp.bfloat16)
    score_qk = jnp.einsum("thd,shd->hts", query_h, key_h, preferred_element_type=jnp.float32)
    weight_qk = jnp.where(allowed[None], score_qk, 0.0).astype(jnp.bfloat16)
    fwd_b = fwd_in.astype(jnp.bfloat16)
    bwd_b = bwd_in.astype(jnp.bfloat16)
    grad_q = jnp.einsum("hts,shd->thd", weight_ov, key_h, preferred_element_type=jnp.float32)
    grad_q = grad_q + first * jnp.einsum(
        "the,hde->thd", grad_h, fwd_b, preferred_element_type=jnp.float32
    )
    grad_q = grad_q.reshape(span, feats).astype(jnp.bfloat16)
    grad_k = jnp.einsum("hts,thd->shd", weight_ov, query_h, preferred_element_type=jnp.float32)
    grad_k = grad_k + last * jnp.einsum(
        "the,hde->thd", value_h, bwd_b, preferred_element_type=jnp.float32
    )
    grad_k = grad_k.reshape(span, feats).astype(jnp.bfloat16)
    grad_v = jnp.einsum("hts,thd->shd", weight_qk, grad_h, preferred_element_type=jnp.float32)
    grad_v = grad_v + last * jnp.einsum(
        "thd,hde->the", key_h, bwd_b, preferred_element_type=jnp.float32
    )
    grad_v = grad_v.reshape(span, feats).astype(jnp.bfloat16)
    count = lax.axis_size("head")
    stacked = jnp.stack([grad_q, grad_k, grad_v], axis=1)
    buffer = place_rows(stacked, owners, count)
    received = lax.all_to_all(buffer, "head", split_axis=0, concat_axis=3, tiled=True)
    return received[0]


def solution(mesh):
    in_specs = (
        P("seq", "head"),
        P("seq", "head"),
        P("seq", "head"),
        P("seq", "head"),
        P("seq"),
        P("seq", None),
    )
    out_specs = P(("seq", "head"), None, None)
    return jax.shard_map(shards, mesh=mesh, in_specs=in_specs, out_specs=out_specs, check_vma=False)
```

profile of v0, /device:TPU:26, one launch (start us, length us, event | category | flops | bytes accessed | tf_op | source)
XLA Modules:
  0.0 590.3 jit_solution(9870636352080246173)
XLA Ops:
  6.5 0.0 copy-start
  6.5 0.0 all-gather.7.cloned.1.call-start
  6.5 1.1 reduce-window.19
  7.7 0.1 slice.19
  7.8 0.1 slice_reduce_fusion.1
  7.9 0.1 fusion.31
  7.9 3.9 copy.85
  11.9 3.9 copy.83
  15.8 3.7 fusion.14
  19.6 0.0 all-gather.7.cloned.1.call-update
  19.6 0.0 all-gather.5.cloned.1.call-start
  19.6 0.6 slice.21
  20.2 3.9 copy.84
  24.2 0.6 fusion.32
  24.8 0.0 copy-done
  24.8 3.2 fusion.11
  27.9 0.0 all-gather.5.cloned.1.call-update
  28.5 0.0 copy-done.7
  28.5 0.7 dynamic-slice
  29.2 0.8 dynamic-update-slice
  30.0 17.2 %all-reduce = f32[8]{0:T(128)S(1)} all-reduce(f32[8]{0:T(128)S(1)} %dynamic-update-slice), channel_id=1, replica_groups=mesh['seq'=8,'head'=4] {'seq'}, use_global_device_ids=true, to_apply=%add | all-reduce | flops 8 | bytes 64
  47.2 0.0 copy-done.6
  47.3 1.1 reduce-window.15
  48.4 0.2 slice_reduce_fusion
  48.6 0.2 reduce-window.16
  48.8 0.1 add_bitcast_fusion
  48.9 0.6 fusion.8
  49.5 0.0 copy-start.4
  49.5 0.0 copy-start.2
  49.5 10.6 %select_convert_fusion.1 = bf16[8,1024,1024]{2,1,0:T(8,128)(2,1)} fusion(pred[1024,1024]{1,0:T(8,128)(4,1)S(1)} %fusion.8, bf16[1024,8,128]{0,2,1:T(8,128)(2,1)} %bitcast.118, bf16[1024,1024]{1,0:T(8,128)(2,1)S(1)} %copy-done), kind=kOutput, calls=%fused_computation.6 | convolution fusion | flops 2164260864 | bytes 22020096 | tf_op jit(solution)/shard_map/thd,shd->hts/dot_general | solution.py:65
  60.1 0.0 copy-done.2
  60.1 11.0 %fusion.33 = f32[8,1024,128]{1,2,0:T(8,128)} fusion(bf16[8,1024,1024]{2,1,0:T(8,128)(2,1)} %select_convert_fusion.1, bf16[1024,8,128]{0,2,1:T(8,128)(2,1)S(1)} %bitcast.110), kind=kOutput, calls=%fused_computation.54 | convolution fusion | flops 2147483648 | bytes 23068672 | tf_op jit(solution)/shard_map/hts,shd->thd/dot_general | solution.py:71
  71.1 20.6 %all-gather.7.cloned.1.call-done = f32[64,128,128]{2,1,0:T(8,128)} async-done(((f32[8,128,128]{2,1,0:T(8,128)}), f32[64,128,128]{2,1,0:T(8,128)}) %all-gather.7.cloned.1.call-update) | async-done | bytes 4194320 | tf_op jit(solution)/shard_map/all_gather | solution.py:13
  91.9 2.7 fusion.9
  94.6 2.8 fusion.23
  97.3 68.3 %all-gather.5.cloned.1.call-done = f32[64,128,128]{2,1,0:T(8,128)} async-done(((f32[8,128,128]{2,1,0:T(8,128)}), f32[64,128,128]{2,1,0:T(8,128)}) %all-gather.5.cloned.1.call-update) | async-done | bytes 4194320 | tf_op jit(solution)/shard_map/all_gather | solution.py:13
  165.7 17.8 %while.26 = (s32[]{:T(128)}, f32[8,128,128]{2,1,0:T(8,128)S(1)}, s32[]{:T(128)}, f32[8,8,128,128]{3,2,1,0:T(8,128)}, f32[8,1,1,1]{0,3,2,1:T(1,128)S(1)}, /*index=5*/s32[]{:T(128)}, s32[]{:T(128)}, s32[]{:T(128)}) while((s32[]{:T(128)}, f32[8,128,128]{2,1,0:T(8,128)S(1)}, s32[]{:T(128)}, f32[8,8,128,128]{3,2,1,0:T(8,128)}, ...), condition=%wide.region_6.7_spmd, body=%wide.region_5.6_spmd.sunk | while | flops 262149 | bytes 1573011 | solution.py:22
  165.7 0.6 constant_dynamic-slice_fusion.4
  166.3 1.9 bitcast_add_fusion.7
  168.2 0.6 constant_dynamic-slice_fusion.4
  168.8 1.9 bitcast_add_fusion.7
  170.7 0.6 constant_dynamic-slice_fusion.4
  171.3 1.9 bitcast_add_fusion.7
  173.2 0.6 constant_dynamic-slice_fusion.4
  173.9 1.9 bitcast_add_fusion.7
  175.8 0.6 constant_dynamic-slice_fusion.4
  176.4 1.9 bitcast_add_fusion.7
  178.3 0.6 constant_dynamic-slice_fusion.4
  178.9 1.9 bitcast_add_fusion.7
  180.8 0.6 constant_dynamic-slice_fusion.4
  181.4 1.9 bitcast_add_fusion.7
  183.5 12.6 %fusion.5 = bf16[1024,8,128]{0,2,1:T(8,128)(2,1)} fusion(f32[8,128,1024]{2,1,0:T(8,128)} %fusion.23, bf16[1024,8,128]{0,2,1:T(8,128)(2,1)} %bitcast.119, pred[1024,1024]{1,0:T(8,128)(4,1)S(1)} %copy-done.5, bf16[1024,8,128]{0,2,1:T(8,128)(2,1)} %bitcast.114, bf16[1024,8,128]{0,2,1:T(8,128)(2,1)} %bitcast.109, f32[1024]{0:T(1024)S(1)} %get-tuple-element.158), kind=kOutput, calls=%fused_computation.13 | convolution fusion | flops 4314890240 | bytes 13635584 | tf_op jit(solution)/shard_map/hts,thd->shd/dot_general | solution.py:81
  196.1 10.9 %copy.75 = bf16[1024,1,1024]{2,1,0:T(2,128)(2,1)} copy(bf16[1024,1,1024]{0,2,1:T(8,128)(2,1)} %bitcast.121) | data formatting | bytes 4194304 | tf_op jit(solution)/shard_map/convert_element_type | solution.py:85
  206.9 11.3 %fusion.6 = bf16[1024,8,128]{0,2,1:T(8,128)(2,1)} fusion(f32[8,128,1024]{2,1,0:T(8,128)} %fusion.9, bf16[1024,8,128]{0,2,1:T(8,128)(2,1)} %bitcast.115, bf16[8,1024,1024]{2,1,0:T(8,128)(2,1)} %select_convert_fusion.1, f32[1024]{0:T(1024)S(1)} %get-tuple-element.158), kind=kOutput, calls=%fused_computation.15 | convolution fusion | flops 2150629376 | bytes 25169920 | tf_op jit(solution)/shard_map/hts,thd->shd/dot_general | solution.py:76
  218.2 10.8 %copy.74 = bf16[1024,1,1024]{2,1,0:T(2,128)(2,1)} copy(bf16[1024,1,1024]{0,2,1:T(8,128)(2,1)} %bitcast.112) | data formatting | bytes 4194304 | tf_op jit(solution)/shard_map/convert_element_type | solution.py:80
  229.0 4.9 fusion.7
  233.9 10.9 %copy.73 = bf16[1024,1,1024]{2,1,0:T(2,128)(2,1)} copy(bf16[1024,1,1024]{0,2,1:T(8,128)(2,1)} %bitcast.116) | data formatting | bytes 4194304 | tf_op jit(solution)/shard_map/convert_element_type | solution.py:75
  244.8 16.9 %pad_maximum_fusion = bf16[1024,3,1024]{2,1,0:T(4,128)(2,1)} fusion(bf16[1024,1,1024]{2,1,0:T(2,128)(2,1)} %copy.75, bf16[1024,1,1024]{2,1,0:T(2,128)(2,1)} %copy.74, bf16[1024,1,1024]{2,1,0:T(2,128)(2,1)} %copy.73), kind=kLoop, calls=%fused_computation.10 | loop fusion | flops 18874368 | bytes 12582912 | tf_op jit(solution)/shard_map/stack | solution.py:87
  261.7 6.0 %broadcast_in_dim.32 = bf16[2048,3,1024]{2,1,0:T(4,128)(2,1)} broadcast(bf16[]{:T(256)} %constant.67.clone.1), dimensions={} | broadcast | bytes 12582914 | tf_op jit(solution)/shard_map/broadcast_in_dim | solution.py:37
  267.7 128.3 %scatter_fusion = bf16[2048,3,1024]{2,1,0:T(4,128)(2,1)} fusion(bf16[2048,3,1024]{2,1,0:T(4,128)(2,1)} %broadcast_in_dim.32, s32[1024]{0:T(1024)S(1)} %bitcast.127, bf16[1024,3,1024]{2,1,0:T(4,128)(2,1)} %pad_maximum_fusion), kind=kCustom, calls=%fused_computation | custom fusion | bytes 18878464 | tf_op jit(solution)/shard_map/scatter | solution.py:37
  396.0 11.7 %copy.77 = bf16[4,512,3,1024]{3,1,2,0:T(8,128)(2,1)S(1)} copy(bf16[4,512,3,1024]{3,2,1,0:T(4,128)(2,1)} %bitcast.106) | data formatting | bytes 25165824 | tf_op jit(solution)/shard_map/reshape | solution.py:38
  407.7 142.2 %all_to_all.15 = bf16[4,512,3,1024]{3,1,2,0:T(8,128)(2,1)} all-to-all(bf16[4,512,3,1024]{3,1,2,0:T(8,128)(2,1)S(1)} %copy.77), channel_id=1, replica_groups=mesh['seq'=8,'head'=4] {'head'}, dimensions={0} | all-to-all | bytes 25165824 | tf_op jit(solution)/shard_map/all_to_all | solution.py:89
  549.9 16.6 %copy.78 = bf16[4,512,3,1024]{1,3,0,2:T(8,128)(2,1)} copy(bf16[4,512,3,1024]{3,1,2,0:T(8,128)(2,1)} %all_to_all.15) | data formatting | bytes 25165824 | tf_op jit(solution)/shard_map/all_to_all | solution.py:89
  566.5 17.0 %copy.79 = bf16[512,3,4096]{2,0,1:T(8,128)(2,1)} copy(bf16[512,3,4096]{0,2,1:T(8,128)(2,1)} %bitcast.107) | data formatting | bytes 25165824 | tf_op jit(solution)/shard_map/squeeze | solution.py:90
  (17 shorter events, 0.2 us)
Async XLA Ops:
  6.5 18.2 %copy-start = (bf16[1024,1024]{1,0:T(8,128)(2,1)S(1)}, bf16[1024,1024]{1,0:T(8,128)(2,1)}, u32[]{:S(2)}) copy-start(bf16[1024,1024]{1,0:T(8,128)(2,1)} %param.12) | copy-start | bytes 6291460
  6.5 85.2 %all-gather.7.cloned.1.call-start = ((), (), s32[]{:S(2)}) async-start(), calls=%async_computation.2 | async-start | bytes 4718592 | tf_op jit(solution)/shard_map/all_gather | solution.py:13
  19.6 146.1 %all-gather.5.cloned.1.call-start = ((), (), s32[]{:S(2)}) async-start(), calls=%async_computation.1 | async-start | bytes 4718592 | tf_op jit(solution)/shard_map/all_gather | solution.py:13
  24.2 4.4 copy-start.7
  24.2 23.1 %copy-start.6 = (s32[1024,1]{0,1:T(1,128)S(1)}, s32[1024,1]{0,1:T(1,128)}, u32[]{:S(2)}) copy-start(s32[1024,1]{0,1:T(1,128)} %param.15) | copy-start | bytes 12292
  49.5 10.6 %copy-start.4 = (pred[1024,1024]{1,0:T(8,128)(4,1)}, pred[1024,1024]{1,0:T(8,128)(4,1)S(1)}, u32[]{:S(2)}) copy-start(pred[1024,1024]{1,0:T(8,128)(4,1)S(1)} %fusion.8) | copy-start | bytes 3145732
  49.5 10.6 %copy-start.2 = (bf16[1024,1024]{0,1:T(8,128)(2,1)S(1)}, bf16[1024,1024]{0,1:T(8,128)(2,1)}, u32[]{:S(2)}) copy-start(bf16[1024,1024]{0,1:T(8,128)(2,1)} %copy.84) | copy-start | bytes 6291460
  91.8 2.7 copy-start.3
  165.6 17.8 %copy-start.5 = (pred[1024,1024]{1,0:T(8,128)(4,1)S(1)}, pred[1024,1024]{1,0:T(8,128)(4,1)}, u32[]{:S(2)}) copy-start(pred[1024,1024]{1,0:T(8,128)(4,1)} %copy-done.4) | copy-start | bytes 3145732
  566.5 17.0 %copy-start.1 = (bf16[1024,1024]{1,0:T(8,128)(2,1)S(1)}, bf16[1024,1024]{1,0:T(8,128)(2,1)}, u32[]{:S(2)}) copy-start(bf16[1024,1024]{1,0:T(8,128)(2,1)} %param.12) | copy-start | bytes 6291460
Sparse Core Ops, SparseCore 0:
  19.7 72.0 all-gather.6
  93.9 71.6 all-gather.4
where the time goes:
time: 594 us; the launch traced here: 590 us
  local copies, waits for them, and re-layouts  231 us (39%)
  blocking collectives  159 us (27%)
  waiting for transfers between devices  89 us (15%)
  matrix products  62.7 us (11%)
  other arithmetic  33.9 us (6%)
  between operations  14.1 us (2%)
    all_to_all x1, blocking collectives, shards(): lax.all_to_all(buffer, 'head', split_axis=0, concat_axis=3, tiled=True)  142 us
    scatter x1, local copies, waits for them, and re-layouts, place_rows(): jnp.zeros((count * capacity,) + block.shape[1:], block.dtype).at[target]  128 us
    all_gather x2, waiting for transfers between devices, entering(): gathered = jax.tree.map(lambda a: lax.all_gather(a, axis), part)  89 us
    unnamed x1, blocking collectives  17.2 us
    squeeze x1, local copies, waits for them, and re-layouts, shards(): return received[0]  17 us
    another operation x1, other arithmetic, shards(): stacked = jnp.stack([grad_q, grad_k, grad_v], axis=1)  16.9 us
    all_to_all x1, local copies, waits for them, and re-layouts, shards(): lax.all_to_all(buffer, 'head', split_axis=0, concat_axis=3, tiled=True)  16.6 us
    add x7, other arithmetic, chain_combine(): return (earlier[0] * later[0], later[1] + later[0] * earlier[1])  13.1 us
  transfers between devices with their start and end apart: 2, of which 2 were waited for; matrix products, arithmetic and copies ran while one was open for 7% of the time, Pallas kernels for 0%

commit v1 on v0

v1 whole, which is shorter than its diff:
```python
import functools

import jax
import jax.numpy as jnp
from jax import lax
from jax.experimental import pallas as pl
from jax.experimental.pallas import tpu as pltpu
from jax.sharding import PartitionSpec as P

HD = 128
TILE = 256
KEEP_ROWS = 16
MESH = pl.DeviceIdType.MESH
F32 = jnp.float32
BF16 = jnp.bfloat16


def dot_nt(a, b):
    return lax.dot_general(a, b, (((1,), (1,)), ((), ())), preferred_element_type=F32)


def dot_tn(a, b):
    return lax.dot_general(a, b, (((0,), (0,)), ((), ())), preferred_element_type=F32)


def dot_nn(a, b):
    return jnp.dot(a, b, preferred_element_type=F32)


def kernel(
    n_seq,
    n_head,
    q_ref,
    k_ref,
    v_ref,
    o_ref,
    starts_ref,
    owners_ref,
    out_ref,
    mask,
    perm,
    first,
    last,
    tot_f,
    tot_b,
    in_f,
    in_b,
    keeps,
    snd,
    rcv,
    grads,
    acc_k,
    acc_v,
    send,
    st_send,
    st_recv,
    out_send,
    out_recv,
    own_sem,
):
    span, feats = q_ref.shape
    heads = feats // HD
    cap = 2 * span // n_head
    steps = n_seq.bit_length() - 1
    me_s = lax.axis_index("seq")
    me_h = lax.axis_index("head")

    def upper(step):
        return lax.rem(lax.div(me_s, 1 << step), 2)

    def partner(step):
        return me_s + (1 << step) * (1 - 2 * upper(step))

    barrier = pltpu.get_barrier_semaphore()
    for step in range(steps):
        pl.semaphore_signal(
            barrier, inc=1, device_id=(partner(step), me_h), device_id_type=MESH
        )
    for off in range(1, n_head):
        pl.semaphore_signal(
            barrier, inc=1, device_id=(me_s, lax.rem(me_h + off, n_head)), device_id_type=MESH
        )

    rows = 16
    row_id = lax.broadcasted_iota(jnp.int32, (rows, span), 0)
    owner = jnp.broadcast_to(owners_ref[...], (rows, span))
    start = jnp.broadcast_to(starts_ref[...], (rows, span)).astype(F32)
    onehot = jnp.where(row_id - 1 == owner, 1.0, 0.0)
    marks = jnp.where(row_id == 0, start, onehot)
    earlier = lax.broadcasted_iota(jnp.int32, (span, span), 0) <= lax.broadcasted_iota(
        jnp.int32, (span, span), 1
    )
    sums = dot_nn(marks.astype(BF16), jnp.where(earlier, 1.0, 0.0).astype(BF16))
    segment = sums[0:1, :]
    slot = jnp.sum(sums * onehot, axis=0, keepdims=True) - 1.0
    target = owners_ref[...] * cap + slot.astype(jnp.int32)
    wide = jnp.broadcast_to(segment, (HD, span)).T
    final = wide[span - 1 : span, :]
    first[...] = jnp.where(wide == 0.0, 1.0, 0.0)
    last[...] = jnp.where(wide == final, 1.0, 0.0)
    keep = jnp.broadcast_to(jnp.where(final == 0.0, 1.0, 0.0), (KEEP_ROWS, HD))
    for tile in range(span // TILE):
        base = tile * TILE
        same = wide[base : base + TILE, 0:1] == segment
        t_id = base + lax.broadcasted_iota(jnp.int32, (TILE, span), 0)
        s_id = lax.broadcasted_iota(jnp.int32, (TILE, span), 1)
        mask[base : base + TILE, :] = jnp.where(same & (s_id <= t_id), 1.0, 0.0)

    def fill(chunk, carry):
        base = pl.multiple_of(chunk * TILE, TILE)
        place = base + lax.broadcasted_iota(jnp.int32, (TILE, span), 0)
        perm[pl.ds(base, TILE), :] = jnp.where(place == target, 1.0, 0.0).astype(BF16)
        return carry

    def state_copy(step, h):
        return pltpu.make_async_remote_copy(
            src_ref=snd.at[step, h],
            dst_ref=rcv.at[step, h],
            send_sem=st_send.at[step, h],
            recv_sem=st_recv.at[step, h],
            device_id=(partner(step), me_h),
            device_id_type=MESH,
        )

    def state_send(step, h):
        snd[step, h, 0:HD, :] = tot_f[h].astype(BF16)
        snd[step, h, HD : 2 * HD, :] = tot_b[h].astype(BF16)
        snd[step, h, 2 * HD :, :] = keeps[h, 0].astype(BF16)
        state_copy(step, h).start()

    def columns(h):
        return pl.ds(pl.multiple_of(h * HD, HD), HD)

    def local_states(h):
        cols = columns(h)
        k_last = (k_ref[:, cols].astype(F32) * last[...]).astype(BF16)
        q_first = (q_ref[:, cols].astype(F32) * first[...]).astype(BF16)
        tot_f[h] = dot_tn(k_last, v_ref[:, cols])
        tot_b[h] = dot_tn(q_first, o_ref[:, cols])
        in_f[h] = jnp.zeros((HD, HD), F32)
        in_b[h] = jnp.zeros((HD, HD), F32)
        keeps[h, 0] = keep
        keeps[h, 1] = jnp.ones((KEEP_ROWS, HD), F32)
        keeps[h, 2] = jnp.ones((KEEP_ROWS, HD), F32)
        state_send(0, h)

    def combine(step, h):
        state_copy(step, h).wait_recv()
        up = jnp.broadcast_to(upper(step), (HD, HD)) == 1
        up_row = up[0:KEEP_ROWS, :]
        got_f = rcv[step, h, 0:HD, :].astype(F32)
        got_b = rcv[step, h, HD : 2 * HD, :].astype(F32)
        got_keep = rcv[step, h, 2 * HD :, :].astype(F32)
        whole, before, after = keeps[h, 0], keeps[h, 1], keeps[h, 2]
        in_f[h] = in_f[h] + jnp.where(up, before[0:1, :] * got_f, 0.0)
        in_b[h] = in_b[h] + jnp.where(up, 0.0, after[0:1, :] * got_b)
        keeps[h, 1] = jnp.where(up_row, before * got_keep, before)
        keeps[h, 2] = jnp.where(up_row, after, after * got_keep)
        if step < steps - 1:
            mine_f, mine_b = tot_f[h], tot_b[h]
            own, other = whole[0:1, :], got_keep[0:1, :]
            tot_f[h] = jnp.where(up, mine_f + own * got_f, got_f + other * mine_f)
            tot_b[h] = jnp.where(up, got_b + other * mine_b, mine_b + own * got_b)
            keeps[h, 0] = whole * got_keep
            state_send(step + 1, h)

    def out_columns(source, h):
        return pl.ds(pl.multiple_of((source * heads + h) * HD, HD), HD)

    def out_copy(off, h):
        peer = lax.rem(me_h + off, n_head)
        return pltpu.make_async_remote_copy(
            src_ref=send.at[h, off],
            dst_ref=out_ref.at[:, :, out_columns(me_h, h)],
            send_sem=out_send.at[h, off],
            recv_sem=out_recv.at[h, off],
            device_id=(me_s, peer),
            device_id_type=MESH,
        )

    def own_copy(h):
        return pltpu.make_async_copy(
            send.at[h, 0], out_ref.at[:, :, out_columns(me_h, h)], own_sem.at[h]
        )

    far_first = [n_head // 2] + [o for o in range(1, n_head) if o != n_head // 2] + [0]

    def gradients(h):
        cols = columns(h)
        fwd = in_f[h].astype(BF16)
        bwd = in_b[h].astype(BF16)
        for tile in reversed(range(span // TILE)):
            here = slice(tile * TILE, (tile + 1) * TILE)
            width = (tile + 1) * TILE
            allowed = mask[here, 0:width]
            o_t = o_ref[here, cols]
            q_t = q_ref[here, cols]
            k_s = k_ref[0:width, cols]
            weight = (dot_nt(o_t, v_ref[0:width, cols]) * allowed).astype(BF16)
            grad_q = dot_nn(weight, k_s) + first[here, :] * dot_nt(o_t, fwd)
            grads[here, 0:HD] = grad_q.astype(BF16)
            add_k = dot_tn(weight, q_t)
            weight = (dot_nt(q_t, k_s) * allowed).astype(BF16)
            add_v = dot_tn(weight, o_t)
            if width == span:
                acc_k[...] = add_k
                acc_v[...] = add_v
            else:
                acc_k[0:width, :] += add_k
                acc_v[0:width, :] += add_v
        grad_k = acc_k[...] + last[...] * dot_nt(v_ref[:, cols], bwd)
        grad_v = acc_v[...] + last[...] * dot_nn(k_ref[:, cols], bwd)
        grads[:, HD : 2 * HD] = grad_k.astype(BF16)
        grads[:, 2 * HD :] = grad_v.astype(BF16)
        for off in far_first:
            base = pl.multiple_of(lax.rem(me_h + off, n_head) * cap, cap)
            placed = dot_nn(perm[pl.ds(base, cap), :], grads[...]).astype(BF16)
            for part in range(3):
                send[h, off, part] = placed[:, part * HD : (part + 1) * HD]
            if off == 0:
                own_copy(h).start()
            else:
                out_copy(off, h).start()

    pl.semaphore_wait(barrier, steps + n_head - 1)

    def turn(t, carry):
        for lag in range(steps, -1, -1):
            h = t - lag

            @pl.when((h >= 0) & (h < heads))
            def _():
                if lag == 0:
                    local_states(h)
                else:
                    combine(lag - 1, h)

        @pl.when(t == 1)
        def _():
            lax.fori_loop(0, n_head * cap // TILE, fill, 0)

        @pl.when((t >= steps) & (t - steps < heads))
        def _():
            gradients(t - steps)

        return carry

    lax.fori_loop(0, heads + steps, turn, 0)

    def finish(h, carry):
        for step in range(steps):
            state_copy(step, h).wait_send()
        for off in range(1, n_head):
            out_copy(off, h).wait_send()
            source = lax.rem(me_h + n_head - off, n_head)
            pltpu.make_async_remote_copy(
                src_ref=send.at[h, off],
                dst_ref=out_ref.at[:, :, out_columns(source, h)],
                send_sem=out_send.at[h, off],
                recv_sem=out_recv.at[h, off],
                device_id=(me_s, source),
                device_id_type=MESH,
            ).wait_recv()
        own_copy(h).wait()
        return carry

    lax.fori_loop(0, heads, finish, 0)


def shards(n_seq, n_head, queries, keys, values, out_grad, starts, owners):
    span, feats = queries.shape
    heads = feats // HD
    cap = 2 * span // n_head
    steps = n_seq.bit_length() - 1
    vmem = pl.BlockSpec(memory_space=pltpu.VMEM)
    flops = heads * (10 * span * span * HD + 12 * span * span * HD)
    out = pl.pallas_call(
        functools.partial(kernel, n_seq, n_head),
        out_shape=jax.ShapeDtypeStruct((3, cap, n_head * feats), BF16),
        in_specs=[vmem] * 6,
        out_specs=pl.BlockSpec(memory_space=pl.ANY),
        scratch_shapes=[
            pltpu.VMEM((span, span), F32),
            pltpu.VMEM((n_head * cap, span), BF16),
            pltpu.VMEM((span, HD), F32),
            pltpu.VMEM((span, HD), F32),
            pltpu.VMEM((heads, HD, HD), F32),
            pltpu.VMEM((heads, HD, HD), F32),
            pltpu.VMEM((heads, HD, HD), F32),
            pltpu.VMEM((heads, HD, HD), F32),
            pltpu.VMEM((heads, 3, KEEP_ROWS, HD), F32),
            pltpu.VMEM((steps, heads, 2 * HD + KEEP_ROWS, HD), BF16),
            pltpu.VMEM((steps, heads, 2 * HD + KEEP_ROWS, HD), BF16),
            pltpu.VMEM((span, 3 * HD), BF16),
            pltpu.VMEM((span, HD), F32),
            pltpu.VMEM((span, HD), F32),
            pltpu.VMEM((heads, n_head, 3, cap, HD), BF16),
            pltpu.SemaphoreType.DMA((steps, heads)),
            pltpu.SemaphoreType.DMA((steps, heads)),
            pltpu.SemaphoreType.DMA((heads, n_head)),
            pltpu.SemaphoreType.DMA((heads, n_head)),
            pltpu.SemaphoreType.DMA((heads,)),
        ],
        compiler_params=pltpu.CompilerParams(
            collective_id=0, has_side_effects=True, vmem_limit_bytes=56 * 1024 * 1024
        ),
        cost_estimate=pl.CostEstimate(
            flops=flops, bytes_accessed=22 * span * feats, transcendentals=0
        ),
    )(queries, keys, values, out_grad, starts.reshape(1, span), owners.reshape(1, span))
    return out.transpose(1, 0, 2)


def solution(mesh):
    in_specs = (
        P("seq", "head"),
        P("seq", "head"),
        P("seq", "head"),
        P("seq", "head"),
        P("seq"),
        P("seq", None),
    )
    return jax.shard_map(
        functools.partial(shards, mesh.shape["seq"], mesh.shape["head"]),
        mesh=mesh,
        in_specs=in_specs,
        out_specs=P(("seq", "head"), None, None),
        check_vma=False,
    )
```

time: 594 us -> 169 us (0.28)
  the two profiles are of different devices: /device:TPU:26 before, /device:TPU:1 now
where the time goes in v1:
time: 169 us
  Pallas kernels  158 us (93%)
  local copies, waits for them, and re-layouts  10.7 us (6%)
    pallas_call x1, Pallas kernels, shards(): pl.pallas_call(functools.partial(kernel, n_seq, n_head), out_shape=jax.Sh...  158 us
    unnamed x1, local copies, waits for them, and re-layouts  10.7 us

profile of v1, /device:TPU:1, one launch (start us, length us, event | category | flops | bytes accessed | tf_op | source)
XLA Modules:
  0.0 169.0 jit_solution(9980975855981986339)
XLA Ops:
  0.0 158.3 %shard_map.64 = bf16[3,512,4096]{2,1,0:T(8,128)(2,1)} custom-call(bf16[1024,1024]{1,0:T(8,128)(2,1)} %q_ref.1, bf16[1024,1024]{1,0:T(8,128)(2,1)} %k_ref.1, bf16[1024,1024]{1,0:T(8,128)(2,1)} %v_ref.1, bf16[1024,1024]{1,0:T(8,128)(2,1)} %o_ref.1, s32[1,1024]{1,0:T(1,128)} %bitcast.4, s32[1,1024]{1,0:T(1,128)} %bitcast.5), custom_call_target="tpu_custom_call" | custom-call | flops 23622320128 | bytes 23068672 | tf_op jit(solution)/shard_map/pallas_call | solution.py:277
  158.4 10.7 %copy.8 = bf16[512,3,4096]{2,0,1:T(8,128)(2,1)} copy(bf16[512,3,4096]{2,0,1:T(8,128)(2,1)} %bitcast.3) | data formatting | bytes 25165824

commit v2 on v1

--- a/solution.py
+++ b/solution.py
@@ -10,9 +10,14 @@
 HD = 128
 TILE = 256
 KEEP_ROWS = 16
+LIST_SHARE = (13, 16)
 MESH = pl.DeviceIdType.MESH
 F32 = jnp.float32
 BF16 = jnp.bfloat16
+
+
+def list_rows(cap):
+    return 2 * cap * LIST_SHARE[0] // LIST_SHARE[1] // 16 * 16
 
 
 def dot_nt(a, b):
@@ -36,7 +41,10 @@
     o_ref,
     starts_ref,
     owners_ref,
-    out_ref,
+    near_ref,
+    far_ref,
+    rest_ref,
+    info_ref,
     mask,
     perm,
     first,
@@ -51,12 +59,20 @@
     grads,
     acc_k,
     acc_v,
-    send,
+    over,
+    counts,
+    near_buf,
+    far_buf,
     st_send,
     st_recv,
-    out_send,
-    out_recv,
+    near_send,
+    near_recv,
     own_sem,
+    far_send,
+    far_recv,
+    rest_sem,
+    fwd_send,
+    fwd_recv,
 ):
     span, feats = q_ref.shape
     heads = feats // HD
@@ -64,22 +80,27 @@
     steps = n_seq.bit_length() - 1
     me_s = lax.axis_index("seq")
     me_h = lax.axis_index("head")
+    chips = n_head // 2
+    my_chip, my_core = lax.div(me_h, 2), lax.rem(me_h, 2)
+    sibling = me_h + 1 - 2 * my_core
+    listed = list_rows(cap)
 
     def upper(step):
         return lax.rem(lax.div(me_s, 1 << step), 2)
 
     def partner(step):
         return me_s + (1 << step) * (1 - 2 * upper(step))
+
+    def far_peer(co):
+        return 2 * lax.rem(my_chip + co, chips) + my_core
 
     barrier = pltpu.get_barrier_semaphore()
     for step in range(steps):
         pl.semaphore_signal(
             barrier, inc=1, device_id=(partner(step), me_h), device_id_type=MESH
         )
-    for off in range(1, n_head):
-        pl.semaphore_signal(
-            barrier, inc=1, device_id=(me_s, lax.rem(me_h + off, n_head)), device_id_type=MESH
-        )
+    for peer in [sibling] + [far_peer(co) for co in range(1, chips)]:
+        pl.semaphore_signal(barrier, inc=1, device_id=(me_s, peer), device_id_type=MESH)
 
     rows = 16
     row_id = lax.broadcasted_iota(jnp.int32, (rows, span), 0)
@@ -93,7 +114,26 @@
     sums = dot_nn(marks.astype(BF16), jnp.where(earlier, 1.0, 0.0).astype(BF16))
     segment = sums[0:1, :]
     slot = jnp.sum(sums * onehot, axis=0, keepdims=True) - 1.0
-    target = owners_ref[...] * cap + slot.astype(jnp.int32)
+    totals = jnp.broadcast_to(jnp.sum(marks, axis=1, keepdims=True), (rows, span))
+    owner_chip = owner // 2
+    evens = jnp.sum(jnp.where(row_id - 1 == 2 * owner_chip, totals, 0.0), axis=0, keepdims=True)
+    own_row = owners_ref[...]
+    chip_row = own_row // 2
+    odd_row = own_row - 2 * chip_row
+    lift = jnp.where(chip_row == my_chip, cap, evens.astype(jnp.int32))
+    target = chip_row * (2 * cap) + odd_row * lift + slot.astype(jnp.int32)
+    counts[...] = totals[:, 0:HD]
+    full = jnp.zeros((1, HD), F32)
+    for chip in range(chips):
+        pair = counts[2 * chip + 1 : 2 * chip + 2, :] + counts[2 * chip + 2 : 2 * chip + 3, :]
+        full = jnp.maximum(full, jnp.where(pair > listed, 1.0, 0.0))
+    over[...] = jnp.broadcast_to(full, (KEEP_ROWS, HD))
+    lane_row = lax.broadcasted_iota(jnp.int32, (rows, HD), 0)
+    mine = jnp.sum(jnp.where(lane_row - 1 == me_h, counts[...], 0.0), axis=0, keepdims=True)
+    even = jnp.where(lane_row - 1 == me_h - 1, counts[...], 0.0)
+    shift = jnp.sum(even, axis=0, keepdims=True) * my_core.astype(F32)
+    info_ref[8:16, :] = jnp.broadcast_to(shift, (8, HD))
+    info_ref[16:24, :] = jnp.broadcast_to(mine, (8, HD))
     wide = jnp.broadcast_to(segment, (HD, span)).T
     final = wide[span - 1 : span, :]
     first[...] = jnp.where(wide == 0.0, 1.0, 0.0)
@@ -125,7 +165,8 @@
     def state_send(step, h):
         snd[step, h, 0:HD, :] = tot_f[h].astype(BF16)
         snd[step, h, HD : 2 * HD, :] = tot_b[h].astype(BF16)
-        snd[step, h, 2 * HD :, :] = keeps[h, 0].astype(BF16)
+        snd[step, h, 2 * HD : 2 * HD + KEEP_ROWS, :] = keeps[h, 0].astype(BF16)
+        snd[step, h, 2 * HD + KEEP_ROWS :, :] = over[...].astype(BF16)
         state_copy(step, h).start()
 
     def columns(h):
@@ -150,7 +191,8 @@
         up_row = up[0:KEEP_ROWS, :]
         got_f = rcv[step, h, 0:HD, :].astype(F32)
         got_b = rcv[step, h, HD : 2 * HD, :].astype(F32)
-        got_keep = rcv[step, h, 2 * HD :, :].astype(F32)
+        got_keep = rcv[step, h, 2 * HD : 2 * HD + KEEP_ROWS, :].astype(F32)
+        over[...] = jnp.maximum(over[...], rcv[step, h, 2 * HD + KEEP_ROWS :, :].astype(F32))
         whole, before, after = keeps[h, 0], keeps[h, 1], keeps[h, 2]
         in_f[h] = in_f[h] + jnp.where(up, before[0:1, :] * got_f, 0.0)
         in_b[h] = in_b[h] + jnp.where(up, 0.0, after[0:1, :] * got_b)
@@ -164,26 +206,47 @@
             keeps[h, 0] = whole * got_keep
             state_send(step + 1, h)
 
-    def out_columns(source, h):
-        return pl.ds(pl.multiple_of((source * heads + h) * HD, HD), HD)
-
-    def out_copy(off, h):
-        peer = lax.rem(me_h + off, n_head)
+    def near_copy(h):
         return pltpu.make_async_remote_copy(
-            src_ref=send.at[h, off],
-            dst_ref=out_ref.at[:, :, out_columns(me_h, h)],
-            send_sem=out_send.at[h, off],
-            recv_sem=out_recv.at[h, off],
-            device_id=(me_s, peer),
+            src_ref=near_buf.at[h, 1],
+            dst_ref=near_ref.at[my_core, :, :, columns(h)],
+            send_sem=near_send.at[h],
+            recv_sem=near_recv.at[h],
+            device_id=(me_s, sibling),
             device_id_type=MESH,
         )
 
     def own_copy(h):
         return pltpu.make_async_copy(
-            send.at[h, 0], out_ref.at[:, :, out_columns(me_h, h)], own_sem.at[h]
-        )
-
-    far_first = [n_head // 2] + [o for o in range(1, n_head) if o != n_head // 2] + [0]
+            near_buf.at[h, 0], near_ref.at[my_core, :, :, columns(h)], own_sem.at[h]
+        )
+
+    def far_copy(co, h):
+        return pltpu.make_async_remote_copy(
+            src_ref=far_buf.at[h, co - 1, :, 0:listed],
+            dst_ref=far_ref.at[co - 1, my_core, :, :, columns(h)],
+            send_sem=far_send.at[h, co - 1],
+            recv_sem=far_recv.at[h, co - 1],
+            device_id=(me_s, far_peer(co)),
+            device_id_type=MESH,
+        )
+
+    def rest_copy(co, h):
+        return pltpu.make_async_copy(
+            far_buf.at[h, co - 1, :, listed : 2 * cap],
+            rest_ref.at[co - 1, :, :, columns(h)],
+            rest_sem.at[h, co - 1],
+        )
+
+    def pass_on(co, h):
+        return pltpu.make_async_remote_copy(
+            src_ref=far_ref.at[co - 1, my_core, :, :, columns(h)],
+            dst_ref=far_ref.at[co - 1, my_core, :, :, columns(h)],
+            send_sem=fwd_send.at[h, co - 1],
+            recv_sem=fwd_recv.at[h, co - 1],
+            device_id=(me_s, sibling),
+            device_id_type=MESH,
+        )
 
     def gradients(h):
         cols = columns(h)
@@ -212,17 +275,26 @@
         grad_v = acc_v[...] + last[...] * dot_nn(k_ref[:, cols], bwd)
         grads[:, HD : 2 * HD] = grad_k.astype(BF16)
         grads[:, 2 * HD :] = grad_v.astype(BF16)
-        for off in far_first:
-            base = pl.multiple_of(lax.rem(me_h + off, n_head) * cap, cap)
+        for co in range(1, chips):
+            base = pl.multiple_of(lax.rem(my_chip + co, chips) * (2 * cap), 2 * cap)
+            for half in range(2):
+                spot = pl.multiple_of(base + half * cap, cap)
+                placed = dot_nn(perm[pl.ds(spot, cap), :], grads[...]).astype(BF16)
+                for part in range(3):
+                    far_buf[h, co - 1, part, half * cap : (half + 1) * cap] = placed[
+                        :, part * HD : (part + 1) * HD
+                    ]
+            far_copy(co, h).start()
+            rest_copy(co, h).start()
+        for place, peer in ((1, sibling), (0, me_h)):
+            base = pl.multiple_of(peer * cap, cap)
             placed = dot_nn(perm[pl.ds(base, cap), :], grads[...]).astype(BF16)
             for part in range(3):
-                send[h, off, part] = placed[:, part * HD : (part + 1) * HD]
-            if off == 0:
-                own_copy(h).start()
-            else:
-                out_copy(off, h).start()
-
-    pl.semaphore_wait(barrier, steps + n_head - 1)
+                near_buf[h, place, part] = placed[:, part * HD : (part + 1) * HD]
+        near_copy(h).start()
+        own_copy(h).start()
+
+    pl.semaphore_wait(barrier, steps + chips)
 
     def turn(t, carry):
         for lag in range(steps, -1, -1):
@@ -247,24 +319,159 @@
 
     lax.fori_loop(0, heads + steps, turn, 0)
 
+    info_ref[0:8, :] = over[0:8, :]
+
+    def forward(h, carry):
+        for co in range(1, chips):
+            far_copy(co, h).wait_recv()
+            pass_on(co, h).start()
+        return carry
+
+    lax.fori_loop(0, heads, forward, 0)
+
     def finish(h, carry):
         for step in range(steps):
             state_copy(step, h).wait_send()
-        for off in range(1, n_head):
-            out_copy(off, h).wait_send()
-            source = lax.rem(me_h + n_head - off, n_head)
-            pltpu.make_async_remote_copy(
-                src_ref=send.at[h, off],
-                dst_ref=out_ref.at[:, :, out_columns(source, h)],
-                send_sem=out_send.at[h, off],
-                recv_sem=out_recv.at[h, off],
-                device_id=(me_s, source),
-                device_id_type=MESH,
-            ).wait_recv()
+        for co in range(1, chips):
+            far_copy(co, h).wait_send()
+            rest_copy(co, h).wait()
+            pass_on(co, h).wait_send()
+            pass_on(co, h).wait_recv()
+        near_copy(h).wait_send()
+        near_copy(h).wait_recv()
         own_copy(h).wait()
         return carry
 
     lax.fori_loop(0, heads, finish, 0)
+
+
+def rest_kernel(n_head, mine_ref, rest_ref, far_send, far_recv, fwd_send, fwd_recv):
+    chips = n_head // 2
+    me_s = lax.axis_index("seq")
+    me_h = lax.axis_index("head")
+    my_chip, my_core = lax.div(me_h, 2), lax.rem(me_h, 2)
+    sibling = me_h + 1 - 2 * my_core
+
+    def far_peer(co):
+        return 2 * lax.rem(my_chip + co, chips) + my_core
+
+    def far_copy(co):
+        return pltpu.make_async_remote_copy(
+            src_ref=mine_ref.at[co - 1],
+            dst_ref=rest_ref.at[co - 1, my_core],
+            send_sem=far_send.at[co - 1],
+            recv_sem=far_recv.at[co - 1],
+            device_id=(me_s, far_peer(co)),
+            device_id_type=MESH,
+        )
+
+    def pass_on(co):
+        return pltpu.make_async_remote_copy(
+            src_ref=rest_ref.at[co - 1, my_core],
+            dst_ref=rest_ref.at[co - 1, my_core],
+            send_sem=fwd_send.at[co - 1],
+            recv_sem=fwd_recv.at[co - 1],
+            device_id=(me_s, sibling),
+            device_id_type=MESH,
+        )
+
+    barrier = pltpu.get_barrier_semaphore()
+    for peer in [sibling] + [far_peer(co) for co in range(1, chips)]:
+        pl.semaphore_signal(barrier, inc=1, device_id=(me_s, peer), device_id_type=MESH)
+    pl.semaphore_wait(barrier, chips)
+    for co in range(1, chips):
+        far_copy(co).start()
+    for co in range(1, chips):
+        far_copy(co).wait_recv()
+        pass_on(co).start()
+    for co in range(1, chips):
+        far_copy(co).wait_send()
+        pass_on(co).wait_send()
+        pass_on(co).wait_recv()
+
+
+def rest_call(n_head, mine):
+    lists, parts, rows, feats = mine.shape
+    sems = pltpu.SemaphoreType.DMA((lists,))
+    return pl.pallas_call(
+        functools.partial(rest_kernel, n_head),
+        out_shape=jax.ShapeDtypeStruct((lists, 2, parts, rows, feats), BF16),
+        in_specs=[pl.BlockSpec(memory_space=pl.ANY)],
+        out_specs=pl.BlockSpec(memory_space=pl.ANY),
+        scratch_shapes=[sems] * 4,
+        compiler_params=pltpu.CompilerParams(collective_id=1, has_side_effects=True),
+    )(mine)
+
+
+def place_kernel(chip_ref, info_ref, near_ref, *refs):
+    *lists, out_ref, pick = refs
+    cap = out_ref.shape[1]
+    source = pl.program_id(1)
+
+    @pl.when((pl.program_id(0) == 0) & (source == 0) & (pl.program_id(2) == 0))
+    def _():
+        slot = lax.broadcasted_iota(jnp.int32, pick.shape, 0)
+        place = lax.broadcasted_iota(jnp.int32, pick.shape, 1)
+        shift = info_ref[8:9, 0:1].astype(jnp.int32)
+        count = info_ref[16:17, 0:1].astype(jnp.int32)
+        pick[...] = jnp.where((place == slot + shift) & (slot < count), 1.0, 0.0).astype(BF16)
+
+    @pl.when(source < 2)
+    def _():
+        out_ref[...] = near_ref[0]
+
+    @pl.when(source >= 2)
+    def _():
+        base, total = 0, None
+        for ref in lists:
+            rows = ref.shape[3]
+            term = dot_nn(pick[:, base : base + rows], ref[0, 0, 0])
+            total = term if total is None else total + term
+            base += rows
+        out_ref[0] = total.astype(BF16)
+
+
+def place_call(n_head, info, near, *lists):
+    _, parts, cap, feats = near.shape
+    chips = n_head // 2
+    wide = 512
+    blocks = feats // wide
+    chip = lax.div(lax.axis_index("head"), 2).astype(jnp.int32).reshape(1)
+
+    def near_map(part, source, block, chip_ref):
+        here = source < 2
+        return (
+            jnp.where(here, source, 1),
+            part,
+            0,
+            jnp.where(here, block, blocks - 1),
+        )
+
+    def list_map(part, source, block, chip_ref):
+        there = source >= 2
+        place = jnp.where(there, source - 2, 0)
+        return (place // 2, place % 2, part, 0, jnp.where(there, block, 0))
+
+    def out_map(part, source, block, chip_ref):
+        origin = lax.rem(chip_ref[0] + chips - source // 2, chips) * 2 + source % 2
+        return (part, 0, origin * blocks + block)
+
+    return pl.pallas_call(
+        place_kernel,
+        out_shape=jax.ShapeDtypeStruct((parts, cap, n_head * feats), BF16),
+        grid_spec=pltpu.PrefetchScalarGridSpec(
+            num_scalar_prefetch=1,
+            grid=(parts, n_head, blocks),
+            in_specs=[
+                pl.BlockSpec((24, HD), lambda part, source, block, chip_ref: (0, 0)),
+                pl.BlockSpec((1, 1, cap, wide), near_map),
+            ]
+            + [pl.BlockSpec((1, 1, 1, a.shape[3], wide), list_map) for a in lists],
+            out_specs=pl.BlockSpec((1, cap, wide), out_map),
+            scratch_shapes=[pltpu.VMEM((cap, sum(a.shape[3] for a in lists)), BF16)],
+        ),
+        compiler_params=pltpu.CompilerParams(vmem_limit_bytes=58 * 1024 * 1024),
+    )(chip, info, near, *lists)
 
 
 def shards(n_seq, n_head, queries, keys, values, out_grad, starts, owners):
@@ -274,11 +481,19 @@
     steps = n_seq.bit_length() - 1
     vmem = pl.BlockSpec(memory_space=pltpu.VMEM)
     flops = heads * (10 * span * span * HD + 12 * span * span * HD)
-    out = pl.pallas_call(
+    chips = n_head // 2
+    listed = list_rows(cap)
+    hbm = pl.BlockSpec(memory_space=pl.ANY)
+    near, far, rest, info = pl.pallas_call(
         functools.partial(kernel, n_seq, n_head),
-        out_shape=jax.ShapeDtypeStruct((3, cap, n_head * feats), BF16),
+        out_shape=[
+            jax.ShapeDtypeStruct((2, 3, cap, feats), BF16),
+            jax.ShapeDtypeStruct((chips - 1, 2, 3, listed, feats), BF16),
+            jax.ShapeDtypeStruct((chips - 1, 3, 2 * cap - listed, feats), BF16),
+            jax.ShapeDtypeStruct((24, HD), F32),
+        ],
         in_specs=[vmem] * 6,
-        out_specs=pl.BlockSpec(memory_space=pl.ANY),
+        out_specs=[hbm, hbm, hbm, vmem],
         scratch_shapes=[
             pltpu.VMEM((span, span), F32),
             pltpu.VMEM((n_head * cap, span), BF16),
@@ -289,17 +504,25 @@
             pltpu.VMEM((heads, HD, HD), F32),
             pltpu.VMEM((heads, HD, HD), F32),
             pltpu.VMEM((heads, 3, KEEP_ROWS, HD), F32),
-            pltpu.VMEM((steps, heads, 2 * HD + KEEP_ROWS, HD), BF16),
-            pltpu.VMEM((steps, heads, 2 * HD + KEEP_ROWS, HD), BF16),
+            pltpu.VMEM((steps, heads, 2 * HD + 2 * KEEP_ROWS, HD), BF16),
+            pltpu.VMEM((steps, heads, 2 * HD + 2 * KEEP_ROWS, HD), BF16),
             pltpu.VMEM((span, 3 * HD), BF16),
             pltpu.VMEM((span, HD), F32),
             pltpu.VMEM((span, HD), F32),
-            pltpu.VMEM((heads, n_head, 3, cap, HD), BF16),
+            pltpu.VMEM((KEEP_ROWS, HD), F32),
+            pltpu.VMEM((16, HD), F32),
+            pltpu.VMEM((heads, 2, 3, cap, HD), BF16),
+            pltpu.VMEM((heads, chips - 1, 3, 2 * cap, HD), BF16),
             pltpu.SemaphoreType.DMA((steps, heads)),
             pltpu.SemaphoreType.DMA((steps, heads)),
-            pltpu.SemaphoreType.DMA((heads, n_head)),
-            pltpu.SemaphoreType.DMA((heads, n_head)),
             pltpu.SemaphoreType.DMA((heads,)),
+            pltpu.SemaphoreType.DMA((heads,)),
+            pltpu.SemaphoreType.DMA((heads,)),
+            pltpu.SemaphoreType.DMA((heads, chips - 1)),
+            pltpu.SemaphoreType.DMA((heads, chips - 1)),
+            pltpu.SemaphoreType.DMA((heads, chips - 1)),
+            pltpu.SemaphoreType.DMA((heads, chips - 1)),
+            pltpu.SemaphoreType.DMA((heads, chips - 1)),
         ],
         compiler_params=pltpu.CompilerParams(
             collective_id=0, has_side_effects=True, vmem_limit_bytes=56 * 1024 * 1024
@@ -308,6 +531,11 @@
             flops=flops, bytes_accessed=22 * span * feats, transcendentals=0
         ),
     )(queries, keys, values, out_grad, starts.reshape(1, span), owners.reshape(1, span))
+    out = lax.cond(
+        info[0, 0] > 0.0,
+        lambda: place_call(n_head, info, near, far, rest_call(n_head, rest)),
+        lambda: place_call(n_head, info, near, far),
+    )
     return out.transpose(1, 0, 2)
 
 

time: 169 us -> 161 us (0.953)
  local copies, waits for them, and re-layouts: 10.7 us -> 0.51 us
    unnamed x1 -> x0, local copies, waits for them, and re-layouts: 10.7 us -> none
    pallas_call x1 -> x2, Pallas kernels: 158 us -> 159 us  [the longest x1 136 us: shards(): pl.pallas_call(functools.partial(kernel, n_seq, n_head), out_shape=[jax.S...]
where the time goes in v2:
time: 161 us; the launch traced here: 160 us
  Pallas kernels  159 us (99%)
    pallas_call x1, Pallas kernels, shards(): pl.pallas_call(functools.partial(kernel, n_seq, n_head), out_shape=[jax.S...  136 us
    pallas_call x1, Pallas kernels, place_call(): pl.pallas_call(place_kernel, out_shape=jax.ShapeDtypeStruct((parts, cap,...  22.8 us

profile of v2, /device:TPU:1, one launch (start us, length us, event | category | flops | bytes accessed | tf_op | source)
XLA Modules:
  0.0 160.3 jit_solution(17097682355430001967)
XLA Ops:
  0.0 136.3 %shard_map.64 = (bf16[2,3,512,1024]{3,2,1,0:T(8,128)(2,1)}, bf16[1,2,3,832,1024]{4,3,2,1,0:T(8,128)(2,1)}, bf16[1,3,192,1024]{3,2,1,0:T(8,128)(2,1)S(1)}, f32[24,128]{1,0:T(8,128)S(1)}) custom-call(bf16[1024,1024]{1,0:T(8,128)(2,1)} %q_ref.1, bf16[1024,1024]{1,0:T(8,128)(2,1)} %k_ref.1, bf16[1024,1024]{1,0:T(8,128)(2,1)} %v_ref.1, bf16[1024,1024]{1,0:T(8,128)(2,1)} %o_ref.1, ...), custom_call_target="tpu_custom_call" | custom-call | flops 23622320128 | bytes 23068672 | tf_op jit(solution)/shard_map/pallas_call | solution.py:487
  136.3 0.5 slice.3
  137.5 22.8 %conditional.1 = (bf16[3,512,4096]{2,1,0:T(8,128)(2,1)}) conditional(s32[]{:T(128)} %bitcast.4, (f32[24,128]{1,0:T(8,128)S(1)}, bf16[2,3,512,1024]{3,2,1,0:T(8,128)(2,1)}, bf16[1,2,3,832,1024]{4,3,2,1,0:T(8,128)(2,1)}) %tuple.11, (bf16[1,3,192,1024]{3,2,1,0:T(8,128)(2,1)S(1)}, f32[24,128]{1,0:T(8,128)S(1)}, bf16[2,3,512,1024]{3,2,1,0:T(8,128)(2,1)}, ...), branch_computations={%region_0.0_spmd, %region_1.0_spmd} | conditional | flops 8 | bytes 91 | solution.py:534
  137.5 22.8 %branch_0_fun.1 = bf16[3,512,4096]{2,1,0:T(8,128)(2,1)} custom-call(s32[1]{0:T(128)} %bitcast.chip_ref, f32[24,128]{1,0:T(8,128)S(1)} %get-tuple-element.22.info_ref, bf16[2,3,512,1024]{3,2,1,0:T(8,128)(2,1)} %get-tuple-element.23.near_ref, bf16[1,2,3,832,1024]{4,3,2,1,0:T(8,128)(2,1)} %get-tuple-element.24.refs_0_), custom_call_target="tpu_custom_call" | custom-call | tf_op jit(solution)/shard_map/cond/branch_0_fun/pallas_call | solution.py:459

commit v3 on v2

--- a/solution.py
+++ b/solution.py
@@ -61,6 +61,9 @@
     acc_v,
     over,
     counts,
+    seg_col,
+    seg_row,
+    acc_q,
     near_buf,
     far_buf,
     st_send,
@@ -139,12 +142,16 @@
     first[...] = jnp.where(wide == 0.0, 1.0, 0.0)
     last[...] = jnp.where(wide == final, 1.0, 0.0)
     keep = jnp.broadcast_to(jnp.where(final == 0.0, 1.0, 0.0), (KEEP_ROWS, HD))
-    for tile in range(span // TILE):
-        base = tile * TILE
-        same = wide[base : base + TILE, 0:1] == segment
+    seg_col[...] = wide
+    seg_row[...] = jnp.broadcast_to(segment, (8, span))
+
+    def fill_mask(chunk, carry):
+        base = pl.multiple_of(chunk * TILE, TILE)
+        same = seg_col[pl.ds(base, TILE), 0:1] == seg_row[0:1, :]
         t_id = base + lax.broadcasted_iota(jnp.int32, (TILE, span), 0)
         s_id = lax.broadcasted_iota(jnp.int32, (TILE, span), 1)
-        mask[base : base + TILE, :] = jnp.where(same & (s_id <= t_id), 1.0, 0.0)
+        mask[pl.ds(base, TILE), :] = jnp.where(same & (s_id <= t_id), 1.0, 0.0)
+        return carry
 
     def fill(chunk, carry):
         base = pl.multiple_of(chunk * TILE, TILE)
@@ -248,10 +255,8 @@
             device_id_type=MESH,
         )
 
-    def gradients(h):
+    def inner(h):
         cols = columns(h)
-        fwd = in_f[h].astype(BF16)
-        bwd = in_b[h].astype(BF16)
         for tile in reversed(range(span // TILE)):
             here = slice(tile * TILE, (tile + 1) * TILE)
             width = (tile + 1) * TILE
@@ -260,8 +265,7 @@
             q_t = q_ref[here, cols]
             k_s = k_ref[0:width, cols]
             weight = (dot_nt(o_t, v_ref[0:width, cols]) * allowed).astype(BF16)
-            grad_q = dot_nn(weight, k_s) + first[here, :] * dot_nt(o_t, fwd)
-            grads[here, 0:HD] = grad_q.astype(BF16)
+            acc_q[here, :] = dot_nn(weight, k_s)
             add_k = dot_tn(weight, q_t)
             weight = (dot_nt(q_t, k_s) * allowed).astype(BF16)
             add_v = dot_tn(weight, o_t)
@@ -271,6 +275,13 @@
             else:
                 acc_k[0:width, :] += add_k
                 acc_v[0:width, :] += add_v
+
+    def finish_head(h):
+        cols = columns(h)
+        fwd = in_f[h].astype(BF16)
+        bwd = in_b[h].astype(BF16)
+        grad_q = acc_q[...] + first[...] * dot_nt(o_ref[:, cols], fwd)
+        grads[:, 0:HD] = grad_q.astype(BF16)
         grad_k = acc_k[...] + last[...] * dot_nt(v_ref[:, cols], bwd)
         grad_v = acc_v[...] + last[...] * dot_nn(k_ref[:, cols], bwd)
         grads[:, HD : 2 * HD] = grad_k.astype(BF16)
@@ -306,14 +317,22 @@
                     local_states(h)
                 else:
                     combine(lag - 1, h)
+                if lag == steps:
+                    finish_head(h)
+
+        @pl.when(t == 0)
+        def _():
+            lax.fori_loop(0, span // TILE, fill_mask, 0)
 
         @pl.when(t == 1)
         def _():
             lax.fori_loop(0, n_head * cap // TILE, fill, 0)
 
-        @pl.when((t >= steps) & (t - steps < heads))
+        ahead = t - (steps - 1)
+
+        @pl.when((ahead >= 0) & (ahead < heads))
         def _():
-            gradients(t - steps)
+            inner(ahead)
 
         return carry
 
@@ -403,12 +422,16 @@
     )(mine)
 
 
+def source_of(turn):
+    return jnp.where(turn == 1, 2, jnp.where(turn == 2, 1, turn))
+
+
 def place_kernel(chip_ref, info_ref, near_ref, *refs):
     *lists, out_ref, pick = refs
     cap = out_ref.shape[1]
-    source = pl.program_id(1)
-
-    @pl.when((pl.program_id(0) == 0) & (source == 0) & (pl.program_id(2) == 0))
+    source = source_of(pl.program_id(2))
+
+    @pl.when((pl.program_id(0) == 0) & (pl.program_id(1) == 0) & (pl.program_id(2) == 0))
     def _():
         slot = lax.broadcasted_iota(jnp.int32, pick.shape, 0)
         place = lax.broadcasted_iota(jnp.int32, pick.shape, 1)
@@ -438,21 +461,15 @@
     blocks = feats // wide
     chip = lax.div(lax.axis_index("head"), 2).astype(jnp.int32).reshape(1)
 
-    def near_map(part, source, block, chip_ref):
-        here = source < 2
-        return (
-            jnp.where(here, source, 1),
-            part,
-            0,
-            jnp.where(here, block, blocks - 1),
-        )
-
-    def list_map(part, source, block, chip_ref):
-        there = source >= 2
-        place = jnp.where(there, source - 2, 0)
-        return (place // 2, place % 2, part, 0, jnp.where(there, block, 0))
-
-    def out_map(part, source, block, chip_ref):
+    def near_map(part, block, turn, chip_ref):
+        return (jnp.where(turn < 2, 0, 1), part, 0, block)
+
+    def list_map(part, block, turn, chip_ref):
+        place = jnp.maximum(source_of(turn) - 2, jnp.where(turn == 2, 1, 0))
+        return (place // 2, place % 2, part, 0, block)
+
+    def out_map(part, block, turn, chip_ref):
+        source = source_of(turn)
         origin = lax.rem(chip_ref[0] + chips - source // 2, chips) * 2 + source % 2
         return (part, 0, origin * blocks + block)
 
@@ -461,9 +478,9 @@
         out_shape=jax.ShapeDtypeStruct((parts, cap, n_head * feats), BF16),
         grid_spec=pltpu.PrefetchScalarGridSpec(
             num_scalar_prefetch=1,
-            grid=(parts, n_head, blocks),
+            grid=(parts, blocks, n_head),
             in_specs=[
-                pl.BlockSpec((24, HD), lambda part, source, block, chip_ref: (0, 0)),
+                pl.BlockSpec((24, HD), lambda part, block, turn, chip_ref: (0, 0)),
                 pl.BlockSpec((1, 1, cap, wide), near_map),
             ]
             + [pl.BlockSpec((1, 1, 1, a.shape[3], wide), list_map) for a in lists],
@@ -511,6 +528,9 @@
             pltpu.VMEM((span, HD), F32),
             pltpu.VMEM((KEEP_ROWS, HD), F32),
             pltpu.VMEM((16, HD), F32),
+            pltpu.VMEM((span, HD), F32),
+            pltpu.VMEM((8, span), F32),
+            pltpu.VMEM((span, HD), F32),
             pltpu.VMEM((heads, 2, 3, cap, HD), BF16),
             pltpu.VMEM((heads, chips - 1, 3, 2 * cap, HD), BF16),
             pltpu.SemaphoreType.DMA((steps, heads)),

time: 161 us -> 156 us (0.969)
  Pallas kernels: 159 us -> 155 us
    pallas_call x1, Pallas kernels: 136 us -> 134 us  [shards(): pl.pallas_call(functools.partial(kernel, n_seq, n_head), out_shape=[jax.S...]
    pallas_call x1, Pallas kernels: 22.8 us -> 20.7 us  [place_call(): pl.pallas_call(place_kernel, out_shape=jax.ShapeDtypeStruct((parts, cap,...]
where the time goes in v3:
time: 156 us
  Pallas kernels  155 us (99%)
    pallas_call x1, Pallas kernels, shards(): pl.pallas_call(functools.partial(kernel, n_seq, n_head), out_shape=[jax.S...  134 us
    pallas_call x1, Pallas kernels, place_call(): pl.pallas_call(place_kernel, out_shape=jax.ShapeDtypeStruct((parts, cap,...  20.7 us

profile of v3, /device:TPU:1, one launch (start us, length us, event | category | flops | bytes accessed | tf_op | source)
XLA Modules:
  0.0 155.7 jit_solution(7093926930899663588)
XLA Ops:
  0.0 133.8 %shard_map.64 = (bf16[2,3,512,1024]{3,2,1,0:T(8,128)(2,1)}, bf16[1,2,3,832,1024]{4,3,2,1,0:T(8,128)(2,1)}, bf16[1,3,192,1024]{3,2,1,0:T(8,128)(2,1)S(1)}, f32[24,128]{1,0:T(8,128)S(1)}) custom-call(bf16[1024,1024]{1,0:T(8,128)(2,1)} %q_ref.1, bf16[1024,1024]{1,0:T(8,128)(2,1)} %k_ref.1, bf16[1024,1024]{1,0:T(8,128)(2,1)} %v_ref.1, bf16[1024,1024]{1,0:T(8,128)(2,1)} %o_ref.1, ...), custom_call_target="tpu_custom_call" | custom-call | flops 23622320128 | bytes 23068672 | tf_op jit(solution)/shard_map/pallas_call | solution.py:504
  133.8 0.5 slice.3
  135.0 20.8 %conditional.1 = (bf16[3,512,4096]{2,1,0:T(8,128)(2,1)}) conditional(s32[]{:T(128)} %bitcast.4, (f32[24,128]{1,0:T(8,128)S(1)}, bf16[2,3,512,1024]{3,2,1,0:T(8,128)(2,1)}, bf16[1,2,3,832,1024]{4,3,2,1,0:T(8,128)(2,1)}) %tuple.11, (bf16[1,3,192,1024]{3,2,1,0:T(8,128)(2,1)S(1)}, f32[24,128]{1,0:T(8,128)S(1)}, bf16[2,3,512,1024]{3,2,1,0:T(8,128)(2,1)}, ...), branch_computations={%region_0.0_spmd, %region_1.0_spmd} | conditional | flops 8 | bytes 91 | solution.py:554
  135.0 20.7 %branch_0_fun.1 = bf16[3,512,4096]{2,1,0:T(8,128)(2,1)} custom-call(s32[1]{0:T(128)} %bitcast.chip_ref, f32[24,128]{1,0:T(8,128)S(1)} %get-tuple-element.22.info_ref, bf16[2,3,512,1024]{3,2,1,0:T(8,128)(2,1)} %get-tuple-element.23.near_ref, bf16[1,2,3,832,1024]{4,3,2,1,0:T(8,128)(2,1)} %get-tuple-element.24.refs_0_), custom_call_target="tpu_custom_call" | custom-call | tf_op jit(solution)/shard_map/cond/branch_0_fun/pallas_call | solution.py:476

commit v4 on v3

--- a/solution.py
+++ b/solution.py
@@ -41,8 +41,7 @@
     o_ref,
     starts_ref,
     owners_ref,
-    near_ref,
-    far_ref,
+    out_ref,
     rest_ref,
     info_ref,
     mask,
@@ -64,6 +63,8 @@
     seg_col,
     seg_row,
     acc_q,
+    pick,
+    land,
     near_buf,
     far_buf,
     st_send,
@@ -76,6 +77,7 @@
     rest_sem,
     fwd_send,
     fwd_recv,
+    put_sem,
 ):
     span, feats = q_ref.shape
     heads = feats // HD
@@ -213,10 +215,13 @@
             keeps[h, 0] = whole * got_keep
             state_send(step + 1, h)
 
+    def out_columns(source, h):
+        return pl.ds(pl.multiple_of((source * heads + h) * HD, HD), HD)
+
     def near_copy(h):
         return pltpu.make_async_remote_copy(
             src_ref=near_buf.at[h, 1],
-            dst_ref=near_ref.at[my_core, :, :, columns(h)],
+            dst_ref=out_ref.at[:, :, out_columns(me_h, h)],
             send_sem=near_send.at[h],
             recv_sem=near_recv.at[h],
             device_id=(me_s, sibling),
@@ -225,13 +230,13 @@
 
     def own_copy(h):
         return pltpu.make_async_copy(
-            near_buf.at[h, 0], near_ref.at[my_core, :, :, columns(h)], own_sem.at[h]
+            near_buf.at[h, 0], out_ref.at[:, :, out_columns(me_h, h)], own_sem.at[h]
         )
 
     def far_copy(co, h):
         return pltpu.make_async_remote_copy(
             src_ref=far_buf.at[h, co - 1, :, 0:listed],
-            dst_ref=far_ref.at[co - 1, my_core, :, :, columns(h)],
+            dst_ref=land.at[h, co - 1, my_core],
             send_sem=far_send.at[h, co - 1],
             recv_sem=far_recv.at[h, co - 1],
             device_id=(me_s, far_peer(co)),
@@ -245,10 +250,18 @@
             rest_sem.at[h, co - 1],
         )
 
+    def put_copy(co, core, h):
+        source = 2 * lax.rem(my_chip + chips - co, chips) + core
+        return pltpu.make_async_copy(
+            far_buf.at[h, co - 1, :, core * cap : (core + 1) * cap],
+            out_ref.at[:, :, out_columns(source, h)],
+            put_sem.at[h, co - 1, core],
+        )
+
     def pass_on(co, h):
         return pltpu.make_async_remote_copy(
-            src_ref=far_ref.at[co - 1, my_core, :, :, columns(h)],
-            dst_ref=far_ref.at[co - 1, my_core, :, :, columns(h)],
+            src_ref=land.at[h, co - 1, my_core],
+            dst_ref=land.at[h, co - 1, my_core],
             send_sem=fwd_send.at[h, co - 1],
             recv_sem=fwd_recv.at[h, co - 1],
             device_id=(me_s, sibling),
@@ -327,6 +340,12 @@
         @pl.when(t == 1)
         def _():
             lax.fori_loop(0, n_head * cap // TILE, fill, 0)
+            spot = lax.broadcasted_iota(jnp.int32, pick.shape, 0)
+            place = lax.broadcasted_iota(jnp.int32, pick.shape, 1)
+            moved = info_ref[8:9, 0:1].astype(jnp.int32)
+            taken = info_ref[16:17, 0:1].astype(jnp.int32)
+            chosen = (place == spot + moved) & (spot < taken)
+            pick[...] = jnp.where(chosen, 1.0, 0.0).astype(BF16)
 
         ahead = t - (steps - 1)
 
@@ -340,22 +359,42 @@
 
     info_ref[0:8, :] = over[0:8, :]
 
-    def forward(h, carry):
-        for co in range(1, chips):
-            far_copy(co, h).wait_recv()
-            pass_on(co, h).start()
+    def forward(t, carry):
+        @pl.when(t < heads)
+        def _():
+            for co in range(1, chips):
+                far_copy(co, t).wait_recv()
+                pass_on(co, t).start()
+
+        @pl.when(t > 0)
+        def _():
+            h = t - 1
+            for co in range(1, chips):
+                far_copy(co, h).wait_send()
+                rest_copy(co, h).wait()
+                pass_on(co, h).wait_recv()
+                for core in range(2):
+                    rows_in = jnp.concatenate(
+                        [land[h, co - 1, core, part] for part in range(3)], axis=1
+                    )
+                    placed = dot_nn(pick[...], rows_in).astype(BF16)
+                    for part in range(3):
+                        far_buf[h, co - 1, part, core * cap : (core + 1) * cap] = placed[
+                            :, part * HD : (part + 1) * HD
+                        ]
+                    put_copy(co, core, h).start()
+
         return carry
 
-    lax.fori_loop(0, heads, forward, 0)
+    lax.fori_loop(0, heads + 1, forward, 0)
 
     def finish(h, carry):
         for step in range(steps):
             state_copy(step, h).wait_send()
         for co in range(1, chips):
-            far_copy(co, h).wait_send()
-            rest_copy(co, h).wait()
             pass_on(co, h).wait_send()
-            pass_on(co, h).wait_recv()
+            for core in range(2):
+                put_copy(co, core, h).wait()
         near_copy(h).wait_send()
         near_copy(h).wait_recv()
         own_copy(h).wait()
@@ -422,73 +461,58 @@
     )(mine)
 
 
-def source_of(turn):
-    return jnp.where(turn == 1, 2, jnp.where(turn == 2, 1, turn))
-
-
-def place_kernel(chip_ref, info_ref, near_ref, *refs):
-    *lists, out_ref, pick = refs
-    cap = out_ref.shape[1]
-    source = source_of(pl.program_id(2))
-
-    @pl.when((pl.program_id(0) == 0) & (pl.program_id(1) == 0) & (pl.program_id(2) == 0))
+def add_kernel(listed, chip_ref, info_ref, have_ref, rest_ref, out_ref, pick):
+    source = pl.program_id(1)
+
+    @pl.when((pl.program_id(0) == 0) & (source == 0))
     def _():
-        slot = lax.broadcasted_iota(jnp.int32, pick.shape, 0)
-        place = lax.broadcasted_iota(jnp.int32, pick.shape, 1)
-        shift = info_ref[8:9, 0:1].astype(jnp.int32)
-        count = info_ref[16:17, 0:1].astype(jnp.int32)
-        pick[...] = jnp.where((place == slot + shift) & (slot < count), 1.0, 0.0).astype(BF16)
+        spot = lax.broadcasted_iota(jnp.int32, pick.shape, 0)
+        place = listed + lax.broadcasted_iota(jnp.int32, pick.shape, 1)
+        moved = info_ref[8:9, 0:1].astype(jnp.int32)
+        taken = info_ref[16:17, 0:1].astype(jnp.int32)
+        chosen = (place == spot + moved) & (spot < taken)
+        pick[...] = jnp.where(chosen, 1.0, 0.0).astype(BF16)
 
     @pl.when(source < 2)
     def _():
-        out_ref[...] = near_ref[0]
+        out_ref[...] = have_ref[...]
 
     @pl.when(source >= 2)
     def _():
-        base, total = 0, None
-        for ref in lists:
-            rows = ref.shape[3]
-            term = dot_nn(pick[:, base : base + rows], ref[0, 0, 0])
-            total = term if total is None else total + term
-            base += rows
-        out_ref[0] = total.astype(BF16)
-
-
-def place_call(n_head, info, near, *lists):
-    _, parts, cap, feats = near.shape
+        more = dot_nn(pick[...], rest_ref[0, 0, 0])
+        out_ref[0] = (have_ref[0].astype(F32) + more).astype(BF16)
+
+
+def add_call(n_head, listed, info, have, rest):
+    lists, _, parts, rows, feats = rest.shape
+    cap = have.shape[1]
     chips = n_head // 2
-    wide = 512
-    blocks = feats // wide
     chip = lax.div(lax.axis_index("head"), 2).astype(jnp.int32).reshape(1)
 
-    def near_map(part, block, turn, chip_ref):
-        return (jnp.where(turn < 2, 0, 1), part, 0, block)
-
-    def list_map(part, block, turn, chip_ref):
-        place = jnp.maximum(source_of(turn) - 2, jnp.where(turn == 2, 1, 0))
-        return (place // 2, place % 2, part, 0, block)
-
-    def out_map(part, block, turn, chip_ref):
-        source = source_of(turn)
+    def rest_map(part, source, chip_ref):
+        place = jnp.maximum(source - 2, 0)
+        return (place // 2, place % 2, part, 0, 0)
+
+    def out_map(part, source, chip_ref):
         origin = lax.rem(chip_ref[0] + chips - source // 2, chips) * 2 + source % 2
-        return (part, 0, origin * blocks + block)
+        return (part, 0, origin)
 
     return pl.pallas_call(
-        place_kernel,
-        out_shape=jax.ShapeDtypeStruct((parts, cap, n_head * feats), BF16),
+        functools.partial(add_kernel, listed),
+        out_shape=jax.ShapeDtypeStruct(have.shape, BF16),
         grid_spec=pltpu.PrefetchScalarGridSpec(
             num_scalar_prefetch=1,
-            grid=(parts, blocks, n_head),
+            grid=(parts, n_head),
             in_specs=[
-                pl.BlockSpec((24, HD), lambda part, block, turn, chip_ref: (0, 0)),
-                pl.BlockSpec((1, 1, cap, wide), near_map),
-            ]
-            + [pl.BlockSpec((1, 1, 1, a.shape[3], wide), list_map) for a in lists],
-            out_specs=pl.BlockSpec((1, cap, wide), out_map),
-            scratch_shapes=[pltpu.VMEM((cap, sum(a.shape[3] for a in lists)), BF16)],
+                pl.BlockSpec((24, HD), lambda part, source, chip_ref: (0, 0)),
+                pl.BlockSpec((1, cap, feats), out_map),
+                pl.BlockSpec((1, 1, 1, rows, feats), rest_map),
+            ],
+            out_specs=pl.BlockSpec((1, cap, feats), out_map),
+            scratch_shapes=[pltpu.VMEM((cap, rows), BF16)],
         ),
         compiler_params=pltpu.CompilerParams(vmem_limit_bytes=58 * 1024 * 1024),
-    )(chip, info, near, *lists)
+    )(chip, info, have, rest)
 
 
 def shards(n_seq, n_head, queries, keys, values, out_grad, starts, owners):
@@ -501,16 +525,15 @@
     chips = n_head // 2
     listed = list_rows(cap)
     hbm = pl.BlockSpec(memory_space=pl.ANY)
-    near, far, rest, info = pl.pallas_call(
+    out, rest, info = pl.pallas_call(
         functools.partial(kernel, n_seq, n_head),
         out_shape=[
-            jax.ShapeDtypeStruct((2, 3, cap, feats), BF16),
-            jax.ShapeDtypeStruct((chips - 1, 2, 3, listed, feats), BF16),
+            jax.ShapeDtypeStruct((3, cap, n_head * feats), BF16),
             jax.ShapeDtypeStruct((chips - 1, 3, 2 * cap - listed, feats), BF16),
             jax.ShapeDtypeStruct((24, HD), F32),
         ],
         in_specs=[vmem] * 6,
-        out_specs=[hbm, hbm, hbm, vmem],
+        out_specs=[hbm, hbm, vmem],
         scratch_shapes=[
             pltpu.VMEM((span, span), F32),
             pltpu.VMEM((n_head * cap, span), BF16),
@@ -531,6 +554,8 @@
             pltpu.VMEM((span, HD), F32),
             pltpu.VMEM((8, span), F32),
             pltpu.VMEM((span, HD), F32),
+            pltpu.VMEM((cap, listed), BF16),
+            pltpu.VMEM((heads, chips - 1, 2, 3, listed, HD), BF16),
             pltpu.VMEM((heads, 2, 3, cap, HD), BF16),
             pltpu.VMEM((heads, chips - 1, 3, 2 * cap, HD), BF16),
             pltpu.SemaphoreType.DMA((steps, heads)),
@@ -543,9 +568,10 @@
             pltpu.SemaphoreType.DMA((heads, chips - 1)),
             pltpu.SemaphoreType.DMA((heads, chips - 1)),
             pltpu.SemaphoreType.DMA((heads, chips - 1)),
+            pltpu.SemaphoreType.DMA((heads, chips - 1, 2)),
         ],
         compiler_params=pltpu.CompilerParams(
-            collective_id=0, has_side_effects=True, vmem_limit_bytes=56 * 1024 * 1024
+            collective_id=0, has_side_effects=True, vmem_limit_bytes=60 * 1024 * 1024
         ),
         cost_estimate=pl.CostEstimate(
             flops=flops, bytes_accessed=22 * span * feats, transcendentals=0
@@ -553,8 +579,8 @@
     )(queries, keys, values, out_grad, starts.reshape(1, span), owners.reshape(1, span))
     out = lax.cond(
         info[0, 0] > 0.0,
-        lambda: place_call(n_head, info, near, far, rest_call(n_head, rest)),
-        lambda: place_call(n_head, info, near, far),
+        lambda: add_call(n_head, listed, info, out, rest_call(n_head, rest)),
+        lambda: out,
     )
     return out.transpose(1, 0, 2)
 

time: 156 us -> 148 us (0.949)
  Pallas kernels: 155 us -> 136 us
  local copies, waits for them, and re-layouts: 0.51 us -> 11.2 us
    pallas_call x1 -> x0, Pallas kernels: 20.7 us -> none  [place_call(): pl.pallas_call(place_kernel, out_shape=jax.ShapeDtypeStruct((parts, cap,...]
    unnamed x0 -> x1, local copies, waits for them, and re-layouts: none -> 10.7 us
    pallas_call x1, Pallas kernels: 134 us -> 136 us  [shards(): pl.pallas_call(functools.partial(kernel, n_seq, n_head), out_shape=[jax.S...]
where the time goes in v4:
time: 148 us
  Pallas kernels  136 us (92%)
  local copies, waits for them, and re-layouts  11.2 us (8%)
    pallas_call x1, Pallas kernels, shards(): pl.pallas_call(functools.partial(kernel, n_seq, n_head), out_shape=[jax.S...  136 us
    unnamed x1, local copies, waits for them, and re-layouts  10.7 us

profile of v4, /device:TPU:1, one launch (start us, length us, event | category | flops | bytes accessed | tf_op | source)
XLA Modules:
  0.0 147.5 jit_solution(17586040307042702617)
XLA Ops:
  0.0 135.7 %shard_map.64 = (bf16[3,512,4096]{2,1,0:T(8,128)(2,1)}, bf16[1,3,192,1024]{3,2,1,0:T(8,128)(2,1)S(1)}, f32[24,128]{1,0:T(8,128)S(1)}) custom-call(bf16[1024,1024]{1,0:T(8,128)(2,1)} %q_ref.1, bf16[1024,1024]{1,0:T(8,128)(2,1)} %k_ref.1, bf16[1024,1024]{1,0:T(8,128)(2,1)} %v_ref.1, bf16[1024,1024]{1,0:T(8,128)(2,1)} %o_ref.1, s32[1,1024]{1,0:T(1,128)} %bitcast.6, ...), custom_call_target="tpu_custom_call" | custom-call | flops 23622320128 | bytes 23068672 | tf_op jit(solution)/shard_map/pallas_call | solution.py:528
  135.7 0.5 slice.3
  136.9 10.7 %copy.12 = bf16[512,3,4096]{2,0,1:T(8,128)(2,1)} copy(bf16[512,3,4096]{2,0,1:T(8,128)(2,1)} %bitcast.5) | data formatting | bytes 25165824
  (1 shorter events, 0.0 us)

commit v5 on v4

--- a/solution.py
+++ b/solution.py
@@ -35,10 +35,10 @@
 def kernel(
     n_seq,
     n_head,
-    q_ref,
-    k_ref,
-    v_ref,
-    o_ref,
+    q_hbm,
+    k_hbm,
+    v_hbm,
+    o_hbm,
     starts_ref,
     owners_ref,
     out_ref,
@@ -78,6 +78,11 @@
     fwd_send,
     fwd_recv,
     put_sem,
+    q_ref,
+    k_ref,
+    v_ref,
+    o_ref,
+    in_sem,
 ):
     span, feats = q_ref.shape
     heads = feats // HD
@@ -89,6 +94,23 @@
     my_chip, my_core = lax.div(me_h, 2), lax.rem(me_h, 2)
     sibling = me_h + 1 - 2 * my_core
     listed = list_rows(cap)
+
+    def columns(h):
+        return pl.ds(pl.multiple_of(h * HD, HD), HD)
+
+    def loads(h):
+        pairs = ((q_hbm, q_ref), (k_hbm, k_ref), (v_hbm, v_ref), (o_hbm, o_ref))
+        return [
+            pltpu.make_async_copy(a.at[:, columns(h)], b.at[:, columns(h)], in_sem.at[i, h])
+            for i, (a, b) in enumerate(pairs)
+        ]
+
+    def load(h, carry):
+        for copy in loads(h):
+            copy.start()
+        return carry
+
+    lax.fori_loop(0, heads, load, 0)
 
     def upper(step):
         return lax.rem(lax.div(me_s, 1 << step), 2)
@@ -178,10 +200,9 @@
         snd[step, h, 2 * HD + KEEP_ROWS :, :] = over[...].astype(BF16)
         state_copy(step, h).start()
 
-    def columns(h):
-        return pl.ds(pl.multiple_of(h * HD, HD), HD)
-
     def local_states(h):
+        for copy in loads(h):
+            copy.wait()
         cols = columns(h)
         k_last = (k_ref[:, cols].astype(F32) * last[...]).astype(BF16)
         q_first = (q_ref[:, cols].astype(F32) * first[...]).astype(BF16)
@@ -532,7 +553,7 @@
             jax.ShapeDtypeStruct((chips - 1, 3, 2 * cap - listed, feats), BF16),
             jax.ShapeDtypeStruct((24, HD), F32),
         ],
-        in_specs=[vmem] * 6,
+        in_specs=[hbm] * 4 + [vmem] * 2,
         out_specs=[hbm, hbm, vmem],
         scratch_shapes=[
             pltpu.VMEM((span, span), F32),
@@ -569,6 +590,11 @@
             pltpu.SemaphoreType.DMA((heads, chips - 1)),
             pltpu.SemaphoreType.DMA((heads, chips - 1)),
             pltpu.SemaphoreType.DMA((heads, chips - 1, 2)),
+            pltpu.VMEM((span, feats), BF16),
+            pltpu.VMEM((span, feats), BF16),
+            pltpu.VMEM((span, feats), BF16),
+            pltpu.VMEM((span, feats), BF16),
+            pltpu.SemaphoreType.DMA((4, heads)),
         ],
         compiler_params=pltpu.CompilerParams(
             collective_id=0, has_side_effects=True, vmem_limit_bytes=60 * 1024 * 1024

time: 148 us -> 145 us (0.980)
  Pallas kernels: 136 us -> 133 us
    pallas_call x1, Pallas kernels: 136 us -> 133 us  [shards(): pl.pallas_call(functools.partial(kernel, n_seq, n_head), out_shape=[jax.S...]
where the time goes in v5:
time: 145 us
  Pallas kernels  133 us (92%)
  local copies, waits for them, and re-layouts  11.2 us (8%)
    pallas_call x1, Pallas kernels, shards(): pl.pallas_call(functools.partial(kernel, n_seq, n_head), out_shape=[jax.S...  133 us
    unnamed x1, local copies, waits for them, and re-layouts  10.7 us

profile of v5, /device:TPU:1, one launch (start us, length us, event | category | flops | bytes accessed | tf_op | source)
XLA Modules:
  0.0 145.2 jit_solution(17856084242373671938)
XLA Ops:
  0.0 133.3 %shard_map.64 = (bf16[3,512,4096]{2,1,0:T(8,128)(2,1)}, bf16[1,3,192,1024]{3,2,1,0:T(8,128)(2,1)S(1)}, f32[24,128]{1,0:T(8,128)S(1)}) custom-call(bf16[1024,1024]{1,0:T(8,128)(2,1)} %q_hbm.1, bf16[1024,1024]{1,0:T(8,128)(2,1)} %k_hbm.1, bf16[1024,1024]{1,0:T(8,128)(2,1)} %v_hbm.1, bf16[1024,1024]{1,0:T(8,128)(2,1)} %o_hbm.1, s32[1,1024]{1,0:T(1,128)} %bitcast.6, ...), custom_call_target="tpu_custom_call" | custom-call | flops 23622320128 | bytes 23068672 | tf_op jit(solution)/shard_map/pallas_call | solution.py:549
  133.3 0.5 slice.3
  134.5 10.7 %copy.12 = bf16[512,3,4096]{2,0,1:T(8,128)(2,1)} copy(bf16[512,3,4096]{2,0,1:T(8,128)(2,1)} %bitcast.5) | data formatting | bytes 25165824
  (1 shorter events, 0.0 us)
